TPU v7x, 32 devices: a whole 2x2x4 slice. The times are simulated.
32 devices in a mesh: chan: 16 (over z, y, core), loc: 2 (over x).
Axes of the slice: x: 2, y: 2, z: 4, core: 2. Of those that a mesh axis runs over, the one named last changes fastest.
Arguments:
- pixels: bfloat16 [512, 256, 256], P('loc', 'chan'), may hold values from -6 to 6
- patch_mask: int32 [512, 256], P('loc', 'chan'), may hold values 0 or 1
- group_map: int32 [256], replicated, may hold values from 0 to 63, as said below
- embed_weight: bfloat16 [256, 2048], P(None, 'loc'), may hold values from -0.375 to 0.375
- mask_token: bfloat16 [2048], replicated, may hold values from -6 to 6
- chan_embed: bfloat16 [256, 2048], P('chan'), may hold values from -3 to 3
- agg_weight: float32 [256], P('chan'), may hold values from 0.5 to 2
- query_key: bfloat16 [16, 2048], replicated, may hold values from -0.02734375 to 0.02734375
- group_bias: float32 [16, 64], replicated, may hold values from -0.5 to 255
- norm_gain: float32 [2048], replicated, may hold values from 0.25 to 1.75
- head_weight: bfloat16 [2048, 256, 256], P(None, 'chan'), may hold values from -0.125 to 0.125
- head_bias: float32 [256, 256], P('chan'), may hold values from -3 to 3
Outputs:
- rebuilt: bfloat16 [512, 256, 256], P('loc', 'chan')
Inputs may be any that keep to these rules, and one draw needn't show every extreme that they name: `group_map`: the 4 channels of each bundle (channels k * 4 to k * 4 + 3) name at most two distinct groups.
All inputs are finite; a program needn't handle non-finite values. No bound on the sum of `patch_mask` on one device may be relied on, other than what follows from the above.
Results may differ from a plain program's by a relative error of at most 0.0051.
Values may be sent and summed in bfloat16 or wider, within the bound.
No kernel may reach another device: no remote copies, remote signals or barrier semaphores. Data moves between devices by JAX's collectives and lax.ppermute only.
A program may use at most 128 MiB of HBM per device.

v0:
```python
import functools

import jax
import jax.numpy as jnp
from jax import lax
from jax.experimental import pallas as pl
from jax.experimental.pallas import tpu as pltpu
from jax.sharding import PartitionSpec as P

G = 64
BUNDLE = 4
LANES = 128
VMEM = pl.BlockSpec(memory_space=pltpu.VMEM)
SMEM = pl.BlockSpec(memory_space=pltpu.SMEM)
HBM = pl.BlockSpec(memory_space=pltpu.HBM)
ANY = pl.BlockSpec(memory_space=pl.ANY)
F32, BF16 = jnp.float32, jnp.bfloat16


def dot(left, right, left_dim=1, right_dim=0):
    dims = (((left_dim,), (right_dim,)), ((), ()))
    return lax.dot_general(left, right, dims, preferred_element_type=F32)


def iota(shape, axis):
    return lax.broadcasted_iota(jnp.int32, shape, axis)


def halves(value):
    high = value.astype(BF16)
    return high, (value - high.astype(F32)).astype(BF16)


def gelu(value):
    return 0.5 * value * (1.0 + lax.erf(value * 0.7071067811865476))


def slot_tables(group_map):
    bundled = group_map.reshape(-1, BUNDLE)
    lowest = jnp.min(bundled, axis=1)
    highest = jnp.max(bundled, axis=1)
    slot_index = (bundled != lowest[:, None]).astype(jnp.int32)
    choose = slot_index[:, None, :] == jnp.arange(2, dtype=jnp.int32)[None, :, None]
    slot_group = jnp.stack([lowest, highest], axis=1).reshape(-1)
    to_group = jnp.arange(G, dtype=jnp.int32)[:, None] == slot_group[None, :]
    return (choose.astype(BF16), to_group.astype(BF16))


def attend(aggregate, query_key, group_bias, norm_gain):
    rows, _, features = aggregate.shape
    heads = query_key.shape[0]
    high = lax.Precision.HIGHEST
    scores = jnp.einsum("lge,he->lhg", aggregate, query_key.astype(F32), precision=high)
    weights = jax.nn.softmax(scores + group_bias[None], axis=-1)
    split = aggregate.reshape(rows, G, heads, features // heads)
    pooled = jnp.einsum("lhg,lghd->lhd", weights, split, precision=high).reshape(rows, features)
    inverse_rms = lax.rsqrt(jnp.mean(pooled * pooled, axis=-1, keepdims=True) + 1e-06)
    return (pooled * inverse_rms * norm_gain[None]).astype(BF16)


def gathered(value, axis, dim):
    count = lax.axis_size(axis)
    copies = jnp.broadcast_to(value[None], (count,) + value.shape)
    parts = lax.all_to_all(copies, axis, split_axis=0, concat_axis=0, tiled=True)
    parts = jnp.moveaxis(parts, 0, dim)
    return parts.reshape(value.shape[:dim] + (-1,) + value.shape[dim + 1 :])


def plain_join(
    pixels, patch_mask, group_map, embed_weight, mask_token, chan_embed, agg_weight, query_key, group_bias, norm_gain
):
    pixel_count = pixels.shape[2]
    choose, to_group = slot_tables(group_map)
    source_pixels = lax.all_to_all(pixels, "chan", split_axis=0, concat_axis=1, tiled=True)
    source_mask = lax.all_to_all(patch_mask, "chan", split_axis=0, concat_axis=1, tiled=True)
    offsets = gathered(chan_embed, "chan", 0).astype(F32)
    weights = gathered(agg_weight, "chan", 0)
    section = gathered(embed_weight, "loc", 1)
    rows, channels, _ = source_pixels.shape
    features = section.shape[1]
    projected = jnp.dot(source_pixels.reshape(rows * channels, pixel_count), section, preferred_element_type=F32)
    projected = projected.reshape(rows, channels, features)
    hidden = source_mask.reshape(rows, channels, 1) == 1
    pre = jnp.where(hidden, mask_token.astype(F32)[None, None, :], projected) + offsets[None]
    weighted = (jax.nn.gelu(pre, approximate=False) * weights[None, :, None]).astype(BF16)
    bundled = weighted.reshape(rows, channels // BUNDLE, BUNDLE, features)
    sums = jnp.einsum("lbke,bsk->lbse", bundled, choose, preferred_element_type=F32)
    sums = sums.reshape(rows, channels // BUNDLE * 2, features).astype(BF16)
    aggregate = jnp.einsum("gq,lqe->lge", to_group, sums, preferred_element_type=F32)
    return attend(aggregate, query_key, group_bias, norm_gain)


def plain_shards(
    pixels,
    patch_mask,
    group_map,
    embed_weight,
    mask_token,
    chan_embed,
    agg_weight,
    query_key,
    group_bias,
    norm_gain,
    head_weight,
    head_bias,
):
    _, own_channels, pixel_count = pixels.shape
    joined = plain_join(
        pixels, patch_mask, group_map, embed_weight, mask_token, chan_embed, agg_weight, query_key, group_bias, norm_gain
    )
    section = gathered(joined, "chan", 0)
    flat_heads = head_weight.reshape(-1, own_channels * pixel_count)
    decoded = jnp.dot(section, flat_heads, preferred_element_type=F32) + head_bias.reshape(1, -1)
    return decoded.astype(BF16).reshape(section.shape[0], own_channels, pixel_count)


def near_flip(block, count):
    quarter = count // 4
    return block // quarter * (count // 2) + (block + 1) % quarter * 2


def pack_kernel(rows, pixels_ref, mask_ref, weight_ref, out_ref):
    peers, pair_rows, width = pixels_ref.shape
    own, locations = mask_ref.shape
    per = locations // peers
    spread = (iota((own, pair_rows), 1) % own == iota((own, pair_rows), 0)).astype(BF16)
    by_location = dot(mask_ref[...].astype(F32).astype(BF16), spread, 0, 0)
    by_location = by_location.reshape(peers, per, pair_rows)
    keep = iota((1, per, pair_rows), 2) // own == iota((1, per, pair_rows), 1)
    hidden = jnp.sum(jnp.where(keep, by_location, 0.0), axis=1)
    visible = 1.0 - hidden
    before = (iota((pair_rows, pair_rows), 0) < iota((pair_rows, pair_rows), 1)).astype(BF16)
    rank = dot(visible.astype(BF16), before)
    place = jnp.where(visible > 0.5, rank, -1.0)
    limit = float(rows - 2)
    over = jnp.max(place, keepdims=True) >= limit
    marked = hidden + jnp.where(over, 2.0, 0.0)
    weight = weight_ref[...]
    high = weight.astype(BF16)
    middle = (weight - high.astype(F32)).astype(BF16)
    low = (weight - high.astype(F32) - middle.astype(F32)).astype(BF16)
    lane = iota((own, width), 1)
    line = iota((own, width), 0)
    weight_row = jnp.zeros((1, width), F32)
    for part, value in enumerate((high, middle, low)):
        weight_row += dot(value, (lane == line + part * own).astype(BF16))
    index = iota((rows, pair_rows), 0).astype(F32)
    for peer in range(peers):
        chosen = (place[peer : peer + 1, :] == index).astype(BF16)
        packed = dot(chosen, pixels_ref[peer])
        line = iota((rows, width), 0)
        mask_row = jnp.pad(marked[peer : peer + 1, :], ((0, 0), (0, width - pair_rows)))
        packed = jnp.where(line == rows - 2, weight_row, packed)
        packed = jnp.where(line == rows - 1, mask_row, packed)
        out_ref[peer] = packed.astype(BF16)


def fetched_rows(start, steps, head_ref, blocks, arrived):
    depth = blocks.shape[1]

    def fetch(step):
        rows = pl.ds(start + step * depth, depth)
        return pltpu.make_async_copy(head_ref.at[rows], blocks.at[step % 2], arrived.at[step % 2])

    fetch(0).start()
    for step in range(steps):
        if step + 1 < steps:
            fetch(step + 1).start()
        fetch(step).wait()
        yield step, blocks[step % 2]


def early_heads_kernel(start, head_ref, out_ref, blocks, turned, arrived, left):
    depth = blocks.shape[1]
    steps = out_ref.shape[1] // depth

    def store(step):
        rows = pl.ds(step * depth, depth)
        return pltpu.make_async_copy(turned.at[step % 2], out_ref.at[:, rows, :], left.at[step % 2])

    for step, rows in fetched_rows(start, steps, head_ref, blocks, arrived):
        if step >= 2:
            store(step - 2).wait()
        turned[step % 2] = jnp.swapaxes(rows, 0, 1)
        store(step).start()
    for step in range(max(steps - 2, 0), steps):
        store(step).wait()


def late_heads_kernel(start, across_ref, head_ref, *refs):
    *most, out_ref, again_ref, over_ref, blocks, arrived = refs
    over_ref[0] = jnp.max(functools.reduce(jnp.maximum, [ref[...] for ref in most]))
    depth = blocks.shape[1]
    again_ref[...] = across_ref[...]
    for step, rows in fetched_rows(start, out_ref.shape[1] // depth, head_ref, blocks, arrived):
        out_ref[:, step * depth : (step + 1) * depth, :] = jnp.swapaxes(rows, 0, 1)


def join_kernel(
    sizes,
    place_ref,
    packed_ref,
    *refs,
):
    sources, own, per, heads, chunk = sizes
    section_refs = refs[: sizes_sections(refs)]
    rest = refs[len(section_refs) :]
    (chan_ref, other_ref, token_ref, query_ref, group_ref, bias_ref, gain_ref, out_ref, over_ref) = rest[:9]
    (embed, offset, table, choice, where, value, score) = rest[9:]
    _, rows, width = packed_ref.shape
    total = sources * rows
    features = embed.shape[1]
    channels = sources * own
    pair_rows = per * own
    depth = features // heads
    chunks = total // chunk

    me_loc = place_ref[0]
    me = place_ref[1]
    sections = len(section_refs)
    part = features // sections
    for step, section in enumerate(section_refs):
        at = lax.rem(me_loc + step, sections) * part
        embed[:, pl.ds(pl.multiple_of(at, part), part)] = section[...]
    half = sources // 2
    for step in range(half):
        for ref, flip in ((chan_ref, 0), (other_ref, 1)):
            source = jnp.bitwise_xor(me, near_flip(step, sources) + flip)
            offset[pl.ds(pl.multiple_of(source * own, own), own), :] = ref[step * own : (step + 1) * own, :]

    last = [packed_ref[s, rows - 16 :, :].astype(F32) for s in range(sources)]
    marked = jnp.concatenate([tail[15:16, :] for tail in last], axis=0)[:, :pair_rows]
    weight_rows = jnp.concatenate([tail[14:15, :] for tail in last], axis=0)
    over = jnp.max((marked >= 2.0).astype(F32), keepdims=True)
    over_ref[...] = jnp.broadcast_to(over, over_ref.shape).astype(jnp.int32)
    hidden = jnp.where(marked >= 2.0, marked - 2.0, marked)
    visible = 1.0 - hidden
    before = (iota((pair_rows, pair_rows), 0) < iota((pair_rows, pair_rows), 1)).astype(BF16)
    rank = dot(visible.astype(BF16), before)
    place = jnp.where(visible > 0.5, rank, -1.0)
    index = iota((rows, pair_rows), 0).astype(F32)
    of_row = iota((pair_rows, LANES), 0) // own
    to_location = (of_row == iota((pair_rows, LANES), 1)).astype(BF16)
    channel_of_row = iota((pair_rows, channels), 0) % own
    for s in range(sources):
        chosen = (place[s : s + 1, :] == index).astype(BF16)
        to_channel = (channel_of_row + s * own == iota((pair_rows, channels), 1)).astype(BF16)
        choice[s * rows : (s + 1) * rows, :] = dot(chosen, to_channel).astype(BF16)
        where[s * rows : (s + 1) * rows, :] = dot(chosen, to_location).astype(BF16)
    lane = iota((width, channels), 0)
    spread = ((lane % own == iota((width, channels), 1) % own) & (lane < 3 * own)).astype(BF16)
    each = dot(weight_rows.astype(BF16), spread)
    mine = iota((sources, channels), 1) // own == iota((sources, channels), 0)
    weight = jnp.sum(jnp.where(mine, each, 0.0), axis=0, keepdims=True)

    block = 256
    for at in range(0, features, block):
        cols = slice(at, at + block)
        table[:, cols] = gelu(token_ref[:, cols].astype(F32) + offset[:, cols].astype(F32)).astype(BF16)
    table_score = dot(query_ref[...], table[...], 1, 1)

    eye = (iota((per, LANES), 0) == iota((per, LANES), 1)).astype(BF16)
    tile = chunk
    counts = jnp.zeros((per, channels), F32)
    spread_score = jnp.zeros((heads * per, channels), F32)
    for c in range(chunks):
        base = c * chunk
        for at in range(0, features, block):
            cols = slice(at, at + block)
            for top in range(base, base + chunk, tile):
                line = slice(top, top + tile)
                pixel = packed_ref[...].reshape(total, width)[line, :]
                pre = dot(pixel, embed[:, cols]) + dot(choice[line, :], offset[:, cols])
                value[line, cols] = gelu(pre).astype(BF16)
        line = slice(base, base + chunk)
        score[c] = dot(query_ref[...], value[line, :], 1, 1)
        at_location = dot(eye, where[line, :], 1, 1)
        counts += dot(at_location.astype(BF16), choice[line, :])
        by_row = [score[c, h : h + 1, :] * at_location for h in range(heads)]
        for piece in halves(jnp.concatenate(by_row, axis=0)):
            spread_score += dot(piece, choice[line, :])

    hidden_at = 1.0 - counts
    by_row = [hidden_at * table_score[h : h + 1, :] for h in range(heads)]
    full = (spread_score + jnp.concatenate(by_row, axis=0)) * weight
    groups = bias_ref.shape[1]
    to_group = (iota((groups, channels), 0) == group_ref[...]).astype(BF16)
    scores = sum(dot(piece, to_group, 1, 1) for piece in halves(full))
    scores += jnp.concatenate([jnp.broadcast_to(bias_ref[h : h + 1, :], (per, groups)) for h in range(heads)], axis=0)
    scores = jnp.exp(scores - jnp.max(scores, axis=-1, keepdims=True))
    attention = scores / jnp.sum(scores, axis=-1, keepdims=True)
    each = sum(dot(piece, to_group) for piece in halves(attention)) * weight

    of_table = halves(each * jnp.concatenate([hidden_at] * heads, axis=0))
    each = halves(each)
    pooled = [jnp.zeros((2 * per, depth), F32)] * heads

    def stack(pieces, h):
        return jnp.concatenate([piece[h * per : (h + 1) * per, :] for piece in pieces], axis=0)

    for h in range(heads):
        pooled[h] += dot(stack(of_table, h), table[:, h * depth : (h + 1) * depth])
    for c in range(chunks):
        line = slice(c * chunk, (c + 1) * chunk)
        at_location = dot(eye, where[line, :], 1, 1)
        spread_each = sum(dot(piece, choice[line, :], 1, 1) for piece in each)
        pieces = halves(spread_each * jnp.concatenate([at_location] * heads, axis=0))
        for h in range(heads):
            pooled[h] += dot(stack(pieces, h), value[line, h * depth : (h + 1) * depth])
    pooled = [both[:per] + both[per:] for both in pooled]
    square = sum(jnp.sum(rows_of * rows_of, axis=-1, keepdims=True) for rows_of in pooled)
    scale = lax.rsqrt(square * (1.0 / features) + 1e-06)
    for h in range(heads):
        cols = slice(h * depth, (h + 1) * depth)
        out_ref[:, cols] = (pooled[h] * scale * gain_ref[:, cols]).astype(BF16)


def sizes_sections(refs):
    return len(refs) - 16


def decode_kernel(place_ref, near_ref, far_ref, low_ref, high_ref, bias_ref, out_ref, joined, decoded):
    own = bias_ref.shape[0]
    half = near_ref.shape[0]
    count, per = out_ref.shape[:2]
    me = place_ref[1]
    split = low_ref.shape[1]
    joined[:half] = near_ref[...]
    joined[half:] = far_ref[...]
    for c in range(own):
        value = dot(joined[:, :split], low_ref[c]) + dot(joined[:, split:], high_ref[c])
        decoded[c] = (value + bias_ref[c : c + 1, :]).astype(BF16)
    for flip in range(2):
        for step in range(half // per):
            owner = jnp.bitwise_xor(me, near_flip(step, count) + flip)
            top = flip * half + step * per
            out_ref[owner] = jnp.swapaxes(decoded[:, top : top + per, :], 0, 1)


def flipped(value, axis, count, flip):
    return lax.ppermute(value, axis, [(i, i ^ flip) for i in range(count)])


def near_rows(value, across, axis, count, again=None):
    near = []
    for rows, own in ((value, value), (across, across if again is None else again)):
        near += [flipped(rows, axis, count, 2 * k) for k in range(1, count // 4)] + [own]
    return jnp.concatenate(near, axis=0)


def shards(
    peers,
    blocks,
    pixels,
    patch_mask,
    group_map,
    embed_weight,
    mask_token,
    chan_embed,
    agg_weight,
    query_key,
    group_bias,
    norm_gain,
    head_weight,
    head_bias,
):
    locations, own, pixel_count = pixels.shape
    channels = group_map.shape[0]
    heads, features = query_key.shape
    per = locations // peers
    pair_rows = per * own
    rows = -(-pair_rows * 3 // 8 // 16) * 16
    total = peers * rows
    fits = (
        peers & (peers - 1) == 0
        and own % 16 == 0
        and per % 16 == 0
        and pair_rows <= pixel_count
        and 3 * own <= pixel_count
        and total % 512 == 0
    )
    if not fits:
        return plain_shards(
            pixels,
            patch_mask,
            group_map,
            embed_weight,
            mask_token,
            chan_embed,
            agg_weight,
            query_key,
            group_bias,
            norm_gain,
            head_weight,
            head_bias,
        )
    vmem = pltpu.CompilerParams(vmem_limit_bytes=24 << 20)
    place = jnp.stack([lax.axis_index("loc"), lax.axis_index("chan")]).astype(jnp.int32)

    packed = pl.pallas_call(
        functools.partial(pack_kernel, rows),
        out_shape=jax.ShapeDtypeStruct((peers, rows, pixel_count), BF16),
        in_specs=[VMEM] * 3,
        out_specs=VMEM,
        compiler_params=vmem,
        name="pack",
    )(pixels.reshape(peers, pair_rows, pixel_count), patch_mask.T, agg_weight.reshape(1, own))
    packed, sent_weight, sent_embed = lax.optimization_barrier((packed, embed_weight, chan_embed))
    packed = lax.all_to_all(packed, "chan", split_axis=0, concat_axis=0, tiled=True)
    sections = [embed_weight]
    for step in range(1, blocks):
        hop = [(i, (i - step) % blocks) for i in range(blocks)]
        sections.append(lax.ppermute(sent_weight, "loc", hop))
    block = features // 8
    split = 6 * block
    turned = [pltpu.VMEM((2, block, own, pixel_count), BF16), pltpu.VMEM((2, own, block, pixel_count), BF16)]
    landed = [pltpu.SemaphoreType.DMA((2,))] * 2
    turn_cost = pl.CostEstimate(flops=0, bytes_accessed=4 * own * split * pixel_count, transcendentals=0)
    across = flipped(sent_embed, "chan", peers, peers // 2)
    across, sent_head = lax.optimization_barrier((across, head_weight))
    early = pl.pallas_call(
        functools.partial(early_heads_kernel, 0),
        out_shape=pltpu.HBM((own, split, pixel_count), BF16),
        in_specs=[ANY],
        out_specs=HBM,
        scratch_shapes=turned + landed,
        compiler_params=vmem,
        cost_estimate=turn_cost,
        name="early_heads",
    )(sent_head)
    near = near_rows(sent_embed, across, "chan", peers)
    near, early = lax.optimization_barrier((near, early))
    far = flipped(near, "chan", peers, 1)
    chunk = 512
    joined, over = pl.pallas_call(
        functools.partial(join_kernel, (peers, own, per, heads, chunk)),
        out_shape=(
            jax.ShapeDtypeStruct((per, features), BF16),
            jax.ShapeDtypeStruct((8, LANES), jnp.int32),
        ),
        in_specs=[SMEM] + [VMEM] * (8 + blocks),
        out_specs=(VMEM, VMEM),
        scratch_shapes=[
            pltpu.VMEM((pixel_count, features), BF16),
            pltpu.VMEM((channels, features), BF16),
            pltpu.VMEM((channels, features), BF16),
            pltpu.VMEM((total, channels), BF16),
            pltpu.VMEM((total, LANES), BF16),
            pltpu.VMEM((total, features), BF16),
            pltpu.VMEM((total // chunk, heads, chunk), F32),
        ],
        compiler_params=vmem,
        cost_estimate=pl.CostEstimate(
            flops=4 * total * features * (pixel_count + 3 * channels),
            bytes_accessed=2 * features * (pixel_count + channels),
            transcendentals=0,
        ),
        name="join",
    )(
        place,
        packed,
        *sections,
        near,
        far,
        mask_token.reshape(1, features),
        query_key,
        group_map.reshape(1, channels),
        group_bias,
        norm_gain.reshape(1, features),
    )
    most = [over]
    for step in range(1, blocks):
        hop = [(i, (i - step) % blocks) for i in range(blocks)]
        most.append(lax.ppermute(over, "loc", hop))
    across = flipped(joined, "chan", peers, peers // 2)
    late, again, over = pl.pallas_call(
        functools.partial(late_heads_kernel, split),
        out_shape=(
            jax.ShapeDtypeStruct((own, features - split, pixel_count), BF16),
            jax.ShapeDtypeStruct((per, features), BF16),
            jax.ShapeDtypeStruct((1,), jnp.int32),
        ),
        in_specs=[VMEM, ANY] + [VMEM] * blocks,
        out_specs=(VMEM, VMEM, SMEM),
        scratch_shapes=turned[:1] + landed[:1],
        compiler_params=vmem,
        cost_estimate=turn_cost,
        name="late_heads",
    )(across, head_weight, *most)
    near = near_rows(joined, across, "chan", peers, again)
    far = flipped(near, "chan", peers, 1)
    rebuilt = pl.pallas_call(
        decode_kernel,
        out_shape=jax.ShapeDtypeStruct((peers, per, own, pixel_count), BF16),
        in_specs=[SMEM] + [VMEM] * 5,
        out_specs=VMEM,
        scratch_shapes=[
            pltpu.VMEM((locations, features), BF16),
            pltpu.VMEM((own, locations, pixel_count), BF16),
        ],
        compiler_params=vmem,
        cost_estimate=pl.CostEstimate(
            flops=2 * locations * features * own * pixel_count,
            bytes_accessed=2 * locations * (features + own * pixel_count),
            transcendentals=0,
        ),
        name="decode",
    )(place, near, far, early, late, head_bias)
    return lax.cond(
        over[0] > 0,
        lambda: plain_shards(
            pixels,
            patch_mask,
            group_map,
            embed_weight,
            mask_token,
            chan_embed,
            agg_weight,
            query_key,
            group_bias,
            norm_gain,
            head_weight,
            head_bias,
        ),
        lambda: rebuilt.reshape(locations, own, pixel_count),
    )


def solution(mesh):
    return jax.shard_map(
        functools.partial(shards, mesh.shape["chan"], mesh.shape["loc"]),
        mesh=mesh,
        in_specs=(
            P("loc", "chan", None),
            P("loc", "chan"),
            P(),
            P(None, "loc"),
            P(),
            P("chan", None),
            P("chan"),
            P(),
            P(),
            P(),
            P(None, "chan", None),
            P("chan", None),
        ),
        out_specs=P("loc", "chan", None),
        check_vma=False,
    )
```

profile of v0, /device:TPU:0, one launch (start us, length us, event | category | flops | bytes accessed | tf_op | source)
XLA Modules:
  0.0 72.8 jit_solution(16106730027118260791)
XLA Ops:
  0.0 3.4 %pack.1 = bf16[16,96,256]{2,1,0:T(8,128)(2,1)} custom-call(bf16[16,256,256]{2,1,0:T(8,128)(2,1)} %bitcast.25.pixels_ref, s32[16,256]{1,0:T(8,128)} %bitcast.103, f32[1,16]{1,0:T(1,128)} %bitcast.108), custom_call_target="tpu_custom_call" | custom-call | tf_op jit(solution)/shard_map/pack/pallas_call | solution.py:400
  3.4 4.0 %collective-permute-start.4 = (bf16[16,2048]{1,0:T(8,128)(2,1)}, bf16[16,2048]{1,0:T(8,128)(2,1)S(1)}, u32[]{:S(2)}, u32[]{:S(2)}) collective-permute-start(bf16[16,2048]{1,0:T(8,128)(2,1)} %param.19), channel_id=1, source_target_pairs={{0,16},{2,18},{4,20},{6,22},{8,24},{10,26},{12,28},{14,30},{16,0},... | collective-permute-start | bytes 196616 | tf_op jit(solution)/shard_map/ppermute | solution.py:341
  7.4 1.5 %collective-permute-start.1 = (bf16[16,2048]{1,0:T(8,128)(2,1)}, bf16[16,2048]{1,0:T(8,128)(2,1)S(1)}, u32[]{:S(2)}, u32[]{:S(2)}) collective-permute-start(bf16[16,2048]{1,0:T(8,128)(2,1)} %param.19), channel_id=1, source_target_pairs={{0,4},{2,6},{4,0},{6,2},{8,12},{10,14},{12,8},{14,10},{16,20},{18,... | collective-permute-start | bytes 196616 | tf_op jit(solution)/shard_map/ppermute | solution.py:341
  9.0 1.6 %collective-permute-start.2 = (bf16[16,2048]{1,0:T(8,128)(2,1)}, bf16[16,2048]{1,0:T(8,128)(2,1)S(1)}, u32[]{:S(2)}, u32[]{:S(2)}) collective-permute-start(bf16[16,2048]{1,0:T(8,128)(2,1)} %param.19), channel_id=1, source_target_pairs={{0,8},{2,10},{4,12},{6,14},{8,0},{10,2},{12,4},{14,6},{16,24},{18,... | collective-permute-start | bytes 196616 | tf_op jit(solution)/shard_map/ppermute | solution.py:341
  10.9 3.9 %all-to-all-start.6 = ((bf16[16,96,256]{2,1,0:T(8,128)(2,1)}), bf16[16,96,256]{2,1,0:T(8,128)(2,1)S(1)}, u32[]{:S(2)}, u32[]{:S(2)}) async-start(bf16[16,96,256]{2,1,0:T(8,128)(2,1)} %pack.1), calls=%async_computation.6 | async-start | bytes 1572864 | tf_op jit(solution)/shard_map/all_to_all | solution.py:409
  14.9 1.6 %collective-permute-start = (bf16[256,1024]{1,0:T(8,128)(2,1)}, bf16[256,1024]{1,0:T(8,128)(2,1)S(1)}, u32[]{:S(2)}, u32[]{:S(2)}) collective-permute-start(bf16[256,1024]{1,0:T(8,128)(2,1)} %refs_0_.1), channel_id=1, source_target_pairs={{0,1},{1,0},{2,3},{3,2},{4,5},{5,4},{6,7},{7,6},{8,9},{9,8},{10,11... | collective-permute-start | bytes 1572872 | tf_op jit(solution)/shard_map/ppermute | solution.py:413
  16.4 1.9 %collective-permute-start.5 = (bf16[16,2048]{1,0:T(8,128)(2,1)S(1)}, bf16[16,2048]{1,0:T(8,128)(2,1)S(1)}, u32[]{:S(2)}, u32[]{:S(2)}) collective-permute-start(bf16[16,2048]{1,0:T(8,128)(2,1)S(1)} %collective-permute-done.4), channel_id=1, source_target_pairs={{0,4},{2,6},{4,0},{6,2},{8,12},{10,14},{12,8},{14,10},{16,20},{18,... | collective-permute-start | bytes 196616 | tf_op jit(solution)/shard_map/ppermute | solution.py:341
  18.3 1.5 %collective-permute-start.6 = (bf16[16,2048]{1,0:T(8,128)(2,1)S(1)}, bf16[16,2048]{1,0:T(8,128)(2,1)S(1)}, u32[]{:S(2)}, u32[]{:S(2)}) collective-permute-start(bf16[16,2048]{1,0:T(8,128)(2,1)S(1)} %collective-permute-done.4), channel_id=1, source_target_pairs={{0,8},{2,10},{4,12},{6,14},{8,0},{10,2},{12,4},{14,6},{16,24},{18,... | collective-permute-start | bytes 196616 | tf_op jit(solution)/shard_map/ppermute | solution.py:341
  20.0 0.8 %constant_dynamic-update-slice_fusion.4 = bf16[128,2048]{1,0:T(8,128)(2,1)S(1)} fusion(bf16[128,2048]{1,0:T(8,128)(2,1)S(1)} %constant_dynamic-update-slice_fusion.5, bf16[16,2048]{1,0:T(8,128)(2,1)} %param.19), kind=kLoop, calls=%fused_computation.61 | loop fusion | bytes 131072
  20.9 11.2 %early_heads.1.low_ref = bf16[16,1536,256]{2,1,0:T(8,128)(2,1)} custom-call(bf16[2048,16,256]{2,1,0:T(8,128)(2,1)} %head_ref.2), custom_call_target="tpu_custom_call" | custom-call | bytes 25165824 | tf_op jit(solution)/shard_map/early_heads/pallas_call | solution.py:421
  32.4 1.8 %collective-permute-done.8.refs_3_ = bf16[128,2048]{1,0:T(8,128)(2,1)S(1)} collective-permute-done((bf16[128,2048]{1,0:T(8,128)(2,1)S(1)}, bf16[128,2048]{1,0:T(8,128)(2,1)S(1)}, u32[]{:S(2)}, u32[]{:S(2)}) %collective-permute-start.8) | collective-permute-done | bytes 524320 | tf_op jit(solution)/shard_map/ppermute | solution.py:341
  34.2 10.4 %join.1 = (bf16[16,2048]{1,0:T(8,128)(2,1)S(1)}, s32[8,128]{1,0:T(8,128)S(1)}) custom-call(s32[2]{0:T(128)S(1)} %pad_add_fusion.1.place_ref, bf16[16,96,256]{2,1,0:T(8,128)(2,1)S(1)} %all-to-all-done.6.packed_ref, bf16[256,1024]{1,0:T(8,128)(2,1)S(1)} %copy-done, bf16[256,1024]{1,0:T(8,128)(2,1)S(1)} %collective-permute-done.refs_1_, ...), custom_call_target="tpu_custom_call" | custom-call | flops 12884901888 | bytes 2097152 | tf_op jit(solution)/shard_map/join/pallas_call | solution.py:435
  44.7 1.9 %collective-permute-start.11 = (bf16[16,2048]{1,0:T(8,128)(2,1)S(1)}, bf16[16,2048]{1,0:T(8,128)(2,1)S(1)}, u32[]{:S(2)}, u32[]{:S(2)}) collective-permute-start(bf16[16,2048]{1,0:T(8,128)(2,1)S(1)} %get-tuple-element.63), channel_id=1, source_target_pairs={{0,4},{2,6},{4,0},{6,2},{8,12},{10,14},{12,8},{14,10},{16,20},{18,... | collective-permute-start | bytes 196616 | tf_op jit(solution)/shard_map/ppermute | solution.py:341
  46.6 3.4 %collective-permute-start.9 = (bf16[16,2048]{1,0:T(8,128)(2,1)S(1)}, bf16[16,2048]{1,0:T(8,128)(2,1)S(1)}, u32[]{:S(2)}, u32[]{:S(2)}) collective-permute-start(bf16[16,2048]{1,0:T(8,128)(2,1)S(1)} %get-tuple-element.63), channel_id=1, source_target_pairs={{0,16},{2,18},{4,20},{6,22},{8,24},{10,26},{12,28},{14,30},{16,0},... | collective-permute-start | bytes 196616 | tf_op jit(solution)/shard_map/ppermute | solution.py:341
  50.0 0.4 collective-permute-start.12
  50.5 3.0 %collective-permute-start.13 = (bf16[16,2048]{1,0:T(8,128)(2,1)S(1)}, bf16[16,2048]{1,0:T(8,128)(2,1)S(1)}, u32[]{:S(2)}, u32[]{:S(2)}) collective-permute-start(bf16[16,2048]{1,0:T(8,128)(2,1)S(1)} %get-tuple-element.63), channel_id=1, source_target_pairs={{0,12},{2,14},{4,8},{6,10},{8,4},{10,6},{12,0},{14,2},{16,28},{18,... | collective-permute-start | bytes 196616 | tf_op jit(solution)/shard_map/ppermute | solution.py:341
  53.5 1.5 %collective-permute-start.10 = (s32[8,128]{1,0:T(8,128)S(1)}, s32[8,128]{1,0:T(8,128)S(1)}, u32[]{:S(2)}, u32[]{:S(2)}) collective-permute-start(s32[8,128]{1,0:T(8,128)S(1)} %get-tuple-element.64.refs_0_), channel_id=1, source_target_pairs={{0,1},{1,0},{2,3},{3,2},{4,5},{5,4},{6,7},{7,6},{8,9},{9,8},{10,11... | collective-permute-start | bytes 12296 | tf_op jit(solution)/shard_map/ppermute | solution.py:474
  55.4 2.0 %collective-permute-done.13 = bf16[16,2048]{1,0:T(8,128)(2,1)S(1)} collective-permute-done((bf16[16,2048]{1,0:T(8,128)(2,1)S(1)}, bf16[16,2048]{1,0:T(8,128)(2,1)S(1)}, u32[]{:S(2)}, u32[]{:S(2)}) %collective-permute-start.13) | collective-permute-done | bytes 65568 | tf_op jit(solution)/shard_map/ppermute | solution.py:341
  57.4 0.9 %collective-permute-start.15 = (bf16[16,2048]{1,0:T(8,128)(2,1)S(1)}, bf16[16,2048]{1,0:T(8,128)(2,1)S(1)}, u32[]{:S(2)}, u32[]{:S(2)}) collective-permute-start(bf16[16,2048]{1,0:T(8,128)(2,1)S(1)} %collective-permute-done.9.across_ref), channel_id=1, source_target_pairs={{0,8},{2,10},{4,12},{6,14},{8,0},{10,2},{12,4},{14,6},{16,24},{18,... | collective-permute-start | bytes 196616 | tf_op jit(solution)/shard_map/ppermute | solution.py:341
  58.3 0.9 %collective-permute-start.16 = (bf16[16,2048]{1,0:T(8,128)(2,1)S(1)}, bf16[16,2048]{1,0:T(8,128)(2,1)S(1)}, u32[]{:S(2)}, u32[]{:S(2)}) collective-permute-start(bf16[16,2048]{1,0:T(8,128)(2,1)S(1)} %collective-permute-done.9.across_ref), channel_id=1, source_target_pairs={{0,12},{2,14},{4,8},{6,10},{8,4},{10,6},{12,0},{14,2},{16,28},{18,... | collective-permute-start | bytes 196616 | tf_op jit(solution)/shard_map/ppermute | solution.py:341
  59.2 2.8 %late_heads.1 = (bf16[16,512,256]{2,1,0:T(8,128)(2,1)S(1)}, bf16[16,2048]{1,0:T(8,128)(2,1)S(1)}, s32[1]{0:T(128)}) custom-call(bf16[16,2048]{1,0:T(8,128)(2,1)S(1)} %collective-permute-done.9.across_ref, bf16[2048,16,256]{2,1,0:T(8,128)(2,1)} %head_ref.2, s32[8,128]{1,0:T(8,128)S(1)} %get-tuple-element.64.refs_0_, s32[8,128]{1,0:T(8,128)S(1)} %collective-permute-done.10.refs_1_), custom_call_target="tpu_custom_call" | custom-call | bytes 25165824 | tf_op jit(solution)/shard_map/late_heads/pallas_call | solution.py:476
  62.1 1.4 %collective-permute-done.16 = bf16[16,2048]{1,0:T(8,128)(2,1)S(1)} collective-permute-done((bf16[16,2048]{1,0:T(8,128)(2,1)S(1)}, bf16[16,2048]{1,0:T(8,128)(2,1)S(1)}, u32[]{:S(2)}, u32[]{:S(2)}) %collective-permute-start.16) | collective-permute-done | bytes 65568 | tf_op jit(solution)/shard_map/ppermute | solution.py:341
  64.2 1.2 %collective-permute-done.17.far_ref = bf16[128,2048]{1,0:T(8,128)(2,1)S(1)} collective-permute-done((bf16[128,2048]{1,0:T(8,128)(2,1)S(1)}, bf16[128,2048]{1,0:T(8,128)(2,1)S(1)}, u32[]{:S(2)}, u32[]{:S(2)}) %collective-permute-start.17) | collective-permute-done | bytes 524320 | tf_op jit(solution)/shard_map/ppermute | solution.py:341
  65.5 6.8 %decode.1 = bf16[16,16,16,256]{3,2,1,0:T(8,128)(2,1)} custom-call(s32[2]{0:T(128)S(1)} %pad_add_fusion.1.place_ref, bf16[128,2048]{1,0:T(8,128)(2,1)S(1)} %constant_dynamic-update-slice_fusion.8.near_ref, bf16[128,2048]{1,0:T(8,128)(2,1)S(1)} %collective-permute-done.17.far_ref, bf16[16,1536,256]{2,1,0:T(8,128)(2,1)S(1)} %bitcast.87, ...), custom_call_target="tpu_custom_call" | custom-call | flops 4294967296 | bytes 3145728 | tf_op jit(solution)/shard_map/decode/pallas_call | solution.py:492
  (65 shorter events, 1.7 us)
Async XLA Ops:
  0.0 34.2 %copy-start = (bf16[256,1024]{1,0:T(8,128)(2,1)S(1)}, bf16[256,1024]{1,0:T(8,128)(2,1)}, u32[]{:S(2)}) copy-start(bf16[256,1024]{1,0:T(8,128)(2,1)} %refs_0_.1) | copy-start | bytes 1572868
  0.0 34.2 %copy-start.2 = (bf16[16,2048]{1,0:T(8,128)(2,1)S(1)}, bf16[16,2048]{1,0:T(8,128)(2,1)}, u32[]{:S(2)}) copy-start(bf16[16,2048]{1,0:T(8,128)(2,1)} %refs_5_.1) | copy-start | bytes 196612
  0.0 34.2 %copy-start.9 = (f32[16,64]{1,0:T(8,128)S(1)}, f32[16,64]{1,0:T(8,128)}, u32[]{:S(2)}) copy-start(f32[16,64]{1,0:T(8,128)} %refs_7_.1) | copy-start | bytes 12292
  0.0 34.2 %copy-start.11 = (f32[2048]{0:T(1024)S(1)}, f32[2048]{0:T(1024)}, u32[]{:S(2)}) copy-start(f32[2048]{0:T(1024)} %param.23) | copy-start | bytes 24580
  0.0 34.2 %copy-start.15 = (s32[256]{0:T(256)S(1)}, s32[256]{0:T(256)}, u32[]{:S(2)}) copy-start(s32[256]{0:T(256)} %param.16) | copy-start | bytes 3076
  3.4 13.0 %collective-permute-start.4 = (bf16[16,2048]{1,0:T(8,128)(2,1)}, bf16[16,2048]{1,0:T(8,128)(2,1)S(1)}, u32[]{:S(2)}, u32[]{:S(2)}) collective-permute-start(bf16[16,2048]{1,0:T(8,128)(2,1)} %param.19), channel_id=1, source_target_pairs={{0,16},{2,18},{4,20},{6,22},{8,24},{10,26},{12,28},{14,30},{16,0},... | collective-permute-start | bytes 196616 | tf_op jit(solution)/shard_map/ppermute | solution.py:341
  7.4 10.8 %collective-permute-start.1 = (bf16[16,2048]{1,0:T(8,128)(2,1)}, bf16[16,2048]{1,0:T(8,128)(2,1)S(1)}, u32[]{:S(2)}, u32[]{:S(2)}) collective-permute-start(bf16[16,2048]{1,0:T(8,128)(2,1)} %param.19), channel_id=1, source_target_pairs={{0,4},{2,6},{4,0},{6,2},{8,12},{10,14},{12,8},{14,10},{16,20},{18,... | collective-permute-start | bytes 196616 | tf_op jit(solution)/shard_map/ppermute | solution.py:341
  9.0 10.8 %collective-permute-start.2 = (bf16[16,2048]{1,0:T(8,128)(2,1)}, bf16[16,2048]{1,0:T(8,128)(2,1)S(1)}, u32[]{:S(2)}, u32[]{:S(2)}) collective-permute-start(bf16[16,2048]{1,0:T(8,128)(2,1)} %param.19), channel_id=1, source_target_pairs={{0,8},{2,10},{4,12},{6,14},{8,0},{10,2},{12,4},{14,6},{16,24},{18,... | collective-permute-start | bytes 196616 | tf_op jit(solution)/shard_map/ppermute | solution.py:341
  10.5 9.5 %collective-permute-start.3 = (bf16[16,2048]{1,0:T(8,128)(2,1)}, bf16[16,2048]{1,0:T(8,128)(2,1)S(1)}, u32[]{:S(2)}, u32[]{:S(2)}) collective-permute-start(bf16[16,2048]{1,0:T(8,128)(2,1)} %param.19), channel_id=1, source_target_pairs={{0,12},{2,14},{4,8},{6,10},{8,4},{10,6},{12,0},{14,2},{16,28},{18,... | collective-permute-start | bytes 196616 | tf_op jit(solution)/shard_map/ppermute | solution.py:341
  10.9 23.3 %all-to-all-start.6 = ((bf16[16,96,256]{2,1,0:T(8,128)(2,1)}), bf16[16,96,256]{2,1,0:T(8,128)(2,1)S(1)}, u32[]{:S(2)}, u32[]{:S(2)}) async-start(bf16[16,96,256]{2,1,0:T(8,128)(2,1)} %pack.1), calls=%async_computation.6 | async-start | bytes 1572864 | tf_op jit(solution)/shard_map/all_to_all | solution.py:409
  14.9 17.5 %collective-permute-start = (bf16[256,1024]{1,0:T(8,128)(2,1)}, bf16[256,1024]{1,0:T(8,128)(2,1)S(1)}, u32[]{:S(2)}, u32[]{:S(2)}) collective-permute-start(bf16[256,1024]{1,0:T(8,128)(2,1)} %refs_0_.1), channel_id=1, source_target_pairs={{0,1},{1,0},{2,3},{3,2},{4,5},{5,4},{6,7},{7,6},{8,9},{9,8},{10,11... | collective-permute-start | bytes 1572872 | tf_op jit(solution)/shard_map/ppermute | solution.py:413
  16.4 15.7 %collective-permute-start.5 = (bf16[16,2048]{1,0:T(8,128)(2,1)S(1)}, bf16[16,2048]{1,0:T(8,128)(2,1)S(1)}, u32[]{:S(2)}, u32[]{:S(2)}) collective-permute-start(bf16[16,2048]{1,0:T(8,128)(2,1)S(1)} %collective-permute-done.4), channel_id=1, source_target_pairs={{0,4},{2,6},{4,0},{6,2},{8,12},{10,14},{12,8},{14,10},{16,20},{18,... | collective-permute-start | bytes 196616 | tf_op jit(solution)/shard_map/ppermute | solution.py:341
  18.3 13.9 %collective-permute-start.6 = (bf16[16,2048]{1,0:T(8,128)(2,1)S(1)}, bf16[16,2048]{1,0:T(8,128)(2,1)S(1)}, u32[]{:S(2)}, u32[]{:S(2)}) collective-permute-start(bf16[16,2048]{1,0:T(8,128)(2,1)S(1)} %collective-permute-done.4), channel_id=1, source_target_pairs={{0,8},{2,10},{4,12},{6,14},{8,0},{10,2},{12,4},{14,6},{16,24},{18,... | collective-permute-start | bytes 196616 | tf_op jit(solution)/shard_map/ppermute | solution.py:341
  19.8 12.4 %collective-permute-start.7 = (bf16[16,2048]{1,0:T(8,128)(2,1)S(1)}, bf16[16,2048]{1,0:T(8,128)(2,1)S(1)}, u32[]{:S(2)}, u32[]{:S(2)}) collective-permute-start(bf16[16,2048]{1,0:T(8,128)(2,1)S(1)} %collective-permute-done.4), channel_id=1, source_target_pairs={{0,12},{2,14},{4,8},{6,10},{8,4},{10,6},{12,0},{14,2},{16,28},{18,... | collective-permute-start | bytes 196616 | tf_op jit(solution)/shard_map/ppermute | solution.py:341
  32.2 2.0 %collective-permute-start.8 = (bf16[128,2048]{1,0:T(8,128)(2,1)S(1)}, bf16[128,2048]{1,0:T(8,128)(2,1)S(1)}, u32[]{:S(2)}, u32[]{:S(2)}) collective-permute-start(bf16[128,2048]{1,0:T(8,128)(2,1)S(1)} %constant_dynamic-update-slice_fusion.refs_2_), channel_id=1, source_target_pairs={{0,2},{2,0},{4,6},{6,4},{8,10},{10,8},{12,14},{14,12},{16,18},{18,... | collective-permute-start | bytes 1572872 | tf_op jit(solution)/shard_map/ppermute | solution.py:341
  44.7 10.2 %collective-permute-start.11 = (bf16[16,2048]{1,0:T(8,128)(2,1)S(1)}, bf16[16,2048]{1,0:T(8,128)(2,1)S(1)}, u32[]{:S(2)}, u32[]{:S(2)}) collective-permute-start(bf16[16,2048]{1,0:T(8,128)(2,1)S(1)} %get-tuple-element.63), channel_id=1, source_target_pairs={{0,4},{2,6},{4,0},{6,2},{8,12},{10,14},{12,8},{14,10},{16,20},{18,... | collective-permute-start | bytes 196616 | tf_op jit(solution)/shard_map/ppermute | solution.py:341
  46.6 8.3 %collective-permute-start.9 = (bf16[16,2048]{1,0:T(8,128)(2,1)S(1)}, bf16[16,2048]{1,0:T(8,128)(2,1)S(1)}, u32[]{:S(2)}, u32[]{:S(2)}) collective-permute-start(bf16[16,2048]{1,0:T(8,128)(2,1)S(1)} %get-tuple-element.63), channel_id=1, source_target_pairs={{0,16},{2,18},{4,20},{6,22},{8,24},{10,26},{12,28},{14,30},{16,0},... | collective-permute-start | bytes 196616 | tf_op jit(solution)/shard_map/ppermute | solution.py:341
  50.0 5.3 %collective-permute-start.12 = (bf16[16,2048]{1,0:T(8,128)(2,1)S(1)}, bf16[16,2048]{1,0:T(8,128)(2,1)S(1)}, u32[]{:S(2)}, u32[]{:S(2)}) collective-permute-start(bf16[16,2048]{1,0:T(8,128)(2,1)S(1)} %get-tuple-element.63), channel_id=1, source_target_pairs={{0,8},{2,10},{4,12},{6,14},{8,0},{10,2},{12,4},{14,6},{16,24},{18,... | collective-permute-start | bytes 196616 | tf_op jit(solution)/shard_map/ppermute | solution.py:341
  50.5 6.9 %collective-permute-start.13 = (bf16[16,2048]{1,0:T(8,128)(2,1)S(1)}, bf16[16,2048]{1,0:T(8,128)(2,1)S(1)}, u32[]{:S(2)}, u32[]{:S(2)}) collective-permute-start(bf16[16,2048]{1,0:T(8,128)(2,1)S(1)} %get-tuple-element.63), channel_id=1, source_target_pairs={{0,12},{2,14},{4,8},{6,10},{8,4},{10,6},{12,0},{14,2},{16,28},{18,... | collective-permute-start | bytes 196616 | tf_op jit(solution)/shard_map/ppermute | solution.py:341
  53.5 5.8 %collective-permute-start.10 = (s32[8,128]{1,0:T(8,128)S(1)}, s32[8,128]{1,0:T(8,128)S(1)}, u32[]{:S(2)}, u32[]{:S(2)}) collective-permute-start(s32[8,128]{1,0:T(8,128)S(1)} %get-tuple-element.64.refs_0_), channel_id=1, source_target_pairs={{0,1},{1,0},{2,3},{3,2},{4,5},{5,4},{6,7},{7,6},{8,9},{9,8},{10,11... | collective-permute-start | bytes 12296 | tf_op jit(solution)/shard_map/ppermute | solution.py:474
  55.0 7.1 %collective-permute-start.14 = (bf16[16,2048]{1,0:T(8,128)(2,1)S(1)}, bf16[16,2048]{1,0:T(8,128)(2,1)S(1)}, u32[]{:S(2)}, u32[]{:S(2)}) collective-permute-start(bf16[16,2048]{1,0:T(8,128)(2,1)S(1)} %collective-permute-done.9.across_ref), channel_id=1, source_target_pairs={{0,4},{2,6},{4,0},{6,2},{8,12},{10,14},{12,8},{14,10},{16,20},{18,... | collective-permute-start | bytes 196616 | tf_op jit(solution)/shard_map/ppermute | solution.py:341
  57.4 4.7 %collective-permute-start.15 = (bf16[16,2048]{1,0:T(8,128)(2,1)S(1)}, bf16[16,2048]{1,0:T(8,128)(2,1)S(1)}, u32[]{:S(2)}, u32[]{:S(2)}) collective-permute-start(bf16[16,2048]{1,0:T(8,128)(2,1)S(1)} %collective-permute-done.9.across_ref), channel_id=1, source_target_pairs={{0,8},{2,10},{4,12},{6,14},{8,0},{10,2},{12,4},{14,6},{16,24},{18,... | collective-permute-start | bytes 196616 | tf_op jit(solution)/shard_map/ppermute | solution.py:341
  58.3 5.2 %collective-permute-start.16 = (bf16[16,2048]{1,0:T(8,128)(2,1)S(1)}, bf16[16,2048]{1,0:T(8,128)(2,1)S(1)}, u32[]{:S(2)}, u32[]{:S(2)}) collective-permute-start(bf16[16,2048]{1,0:T(8,128)(2,1)S(1)} %collective-permute-done.9.across_ref), channel_id=1, source_target_pairs={{0,12},{2,14},{4,8},{6,10},{8,4},{10,6},{12,0},{14,2},{16,28},{18,... | collective-permute-start | bytes 196616 | tf_op jit(solution)/shard_map/ppermute | solution.py:341
  63.5 2.0 %collective-permute-start.17 = (bf16[128,2048]{1,0:T(8,128)(2,1)S(1)}, bf16[128,2048]{1,0:T(8,128)(2,1)S(1)}, u32[]{:S(2)}, u32[]{:S(2)}) collective-permute-start(bf16[128,2048]{1,0:T(8,128)(2,1)S(1)} %constant_dynamic-update-slice_fusion.8.near_ref), channel_id=1, source_target_pairs={{0,2},{2,0},{4,6},{6,4},{8,10},{10,8},{12,14},{14,12},{16,18},{18,... | collective-permute-start | bytes 1572872 | tf_op jit(solution)/shard_map/ppermute | solution.py:341
  (8 other events, 191.5 us)
where the time goes:
time: 73.1 us; the launch traced here: 72.8 us
  Pallas kernels  34.7 us (47%)
  starting transfers between devices  29.2 us (40%)
  waiting for transfers between devices  6.38 us (9%)
  between operations  1.18 us (2%)
  local copies, waits for them, and re-layouts  1.01 us (1%)
    ppermute x16, starting transfers between devices, flipped(): return lax.ppermute(value, axis, [(i, i ^ flip) for i in range(count)])  22.2 us
    pallas_call x1, Pallas kernels, shards(): pl.pallas_call(functools.partial(early_heads_kernel, 0), out_shape=pltpu....  11.2 us
    pallas_call x1, Pallas kernels, shards(): pl.pallas_call(functools.partial(join_kernel, (peers, own, per, heads, ch...  10.4 us
    pallas_call x1, Pallas kernels, shards(): pl.pallas_call(decode_kernel, out_shape=jax.ShapeDtypeStruct((peers, per,...  6.79 us
    ppermute x16, waiting for transfers between devices, flipped(): return lax.ppermute(value, axis, [(i, i ^ flip) for i in range(count)])  6.37 us
    all_to_all x1, starting transfers between devices, shards(): lax.all_to_all(packed, 'chan', split_axis=0, concat_axis=0, tiled=True)  3.91 us
    pallas_call x1, Pallas kernels, shards(): pl.pallas_call(functools.partial(pack_kernel, rows), out_shape=jax.ShapeD...  3.36 us
    pallas_call x1, Pallas kernels, shards(): pl.pallas_call(functools.partial(late_heads_kernel, split), out_shape=(ja...  2.83 us
  transfers between devices with their start and end apart: 19, of which 4 were waited for; matrix products, arithmetic and copies ran while one was open for 1% of the time, Pallas kernels for 19%

commit v1 on v0

--- a/solution.py
+++ b/solution.py
@@ -431,7 +431,7 @@
     near = near_rows(sent_embed, across, "chan", peers)
     near, early = lax.optimization_barrier((near, early))
     far = flipped(near, "chan", peers, 1)
-    chunk = 512
+    chunk = total // 2
     joined, over = pl.pallas_call(
         functools.partial(join_kernel, (peers, own, per, heads, chunk)),
         out_shape=(

time: 73.1 us -> 73.4 us (level)
  no operation moved by 1% of the time
where the time goes in v1:
time: 73.4 us; the launch traced here: 73 us
  Pallas kernels  35 us (48%)
  starting transfers between devices  29.2 us (40%)
  waiting for transfers between devices  6.37 us (9%)
  between operations  1.18 us (2%)
  local copies, waits for them, and re-layouts  1.01 us (1%)
    ppermute x16, starting transfers between devices, flipped(): return lax.ppermute(value, axis, [(i, i ^ flip) for i in range(count)])  22.2 us
    pallas_call x1, Pallas kernels, shards(): pl.pallas_call(functools.partial(early_heads_kernel, 0), out_shape=pltpu....  11.2 us
    pallas_call x1, Pallas kernels, shards(): pl.pallas_call(functools.partial(join_kernel, (peers, own, per, heads, ch...  10.7 us
    pallas_call x1, Pallas kernels, shards(): pl.pallas_call(decode_kernel, out_shape=jax.ShapeDtypeStruct((peers, per,...  6.79 us
    ppermute x16, waiting for transfers between devices, flipped(): return lax.ppermute(value, axis, [(i, i ^ flip) for i in range(count)])  6.36 us
    all_to_all x1, starting transfers between devices, shards(): lax.all_to_all(packed, 'chan', split_axis=0, concat_axis=0, tiled=True)  3.91 us
    pallas_call x1, Pallas kernels, shards(): pl.pallas_call(functools.partial(pack_kernel, rows), out_shape=jax.ShapeD...  3.36 us
    pallas_call x1, Pallas kernels, shards(): pl.pallas_call(functools.partial(late_heads_kernel, split), out_shape=(ja...  2.83 us
  transfers between devices with their start and end apart: 19, of which 4 were waited for; matrix products, arithmetic and copies ran while one was open for 1% of the time, Pallas kernels for 19%

profile of v1, /device:TPU:0, one launch (start us, length us, event | category | flops | bytes accessed | tf_op | source)
XLA Modules:
  0.0 73.0 jit_solution(10739906730376333187)
XLA Ops:
  0.0 3.4 %pack.1 = bf16[16,96,256]{2,1,0:T(8,128)(2,1)} custom-call(bf16[16,256,256]{2,1,0:T(8,128)(2,1)} %bitcast.25.pixels_ref, s32[16,256]{1,0:T(8,128)} %bitcast.103, f32[1,16]{1,0:T(1,128)} %bitcast.108), custom_call_target="tpu_custom_call" | custom-call | tf_op jit(solution)/shard_map/pack/pallas_call | solution.py:400
  3.4 4.0 %collective-permute-start.4 = (bf16[16,2048]{1,0:T(8,128)(2,1)}, bf16[16,2048]{1,0:T(8,128)(2,1)S(1)}, u32[]{:S(2)}, u32[]{:S(2)}) collective-permute-start(bf16[16,2048]{1,0:T(8,128)(2,1)} %param.19), channel_id=1, source_target_pairs={{0,16},{2,18},{4,20},{6,22},{8,24},{10,26},{12,28},{14,30},{16,0},... | collective-permute-start | bytes 196616 | tf_op jit(solution)/shard_map/ppermute | solution.py:341
  7.4 1.5 %collective-permute-start.1 = (bf16[16,2048]{1,0:T(8,128)(2,1)}, bf16[16,2048]{1,0:T(8,128)(2,1)S(1)}, u32[]{:S(2)}, u32[]{:S(2)}) collective-permute-start(bf16[16,2048]{1,0:T(8,128)(2,1)} %param.19), channel_id=1, source_target_pairs={{0,4},{2,6},{4,0},{6,2},{8,12},{10,14},{12,8},{14,10},{16,20},{18,... | collective-permute-start | bytes 196616 | tf_op jit(solution)/shard_map/ppermute | solution.py:341
  9.0 1.6 %collective-permute-start.2 = (bf16[16,2048]{1,0:T(8,128)(2,1)}, bf16[16,2048]{1,0:T(8,128)(2,1)S(1)}, u32[]{:S(2)}, u32[]{:S(2)}) collective-permute-start(bf16[16,2048]{1,0:T(8,128)(2,1)} %param.19), channel_id=1, source_target_pairs={{0,8},{2,10},{4,12},{6,14},{8,0},{10,2},{12,4},{14,6},{16,24},{18,... | collective-permute-start | bytes 196616 | tf_op jit(solution)/shard_map/ppermute | solution.py:341
  10.9 3.9 %all-to-all-start.6 = ((bf16[16,96,256]{2,1,0:T(8,128)(2,1)}), bf16[16,96,256]{2,1,0:T(8,128)(2,1)S(1)}, u32[]{:S(2)}, u32[]{:S(2)}) async-start(bf16[16,96,256]{2,1,0:T(8,128)(2,1)} %pack.1), calls=%async_computation.6 | async-start | bytes 1572864 | tf_op jit(solution)/shard_map/all_to_all | solution.py:409
  14.9 1.6 %collective-permute-start = (bf16[256,1024]{1,0:T(8,128)(2,1)}, bf16[256,1024]{1,0:T(8,128)(2,1)S(1)}, u32[]{:S(2)}, u32[]{:S(2)}) collective-permute-start(bf16[256,1024]{1,0:T(8,128)(2,1)} %refs_0_.1), channel_id=1, source_target_pairs={{0,1},{1,0},{2,3},{3,2},{4,5},{5,4},{6,7},{7,6},{8,9},{9,8},{10,11... | collective-permute-start | bytes 1572872 | tf_op jit(solution)/shard_map/ppermute | solution.py:413
  16.4 1.9 %collective-permute-start.5 = (bf16[16,2048]{1,0:T(8,128)(2,1)S(1)}, bf16[16,2048]{1,0:T(8,128)(2,1)S(1)}, u32[]{:S(2)}, u32[]{:S(2)}) collective-permute-start(bf16[16,2048]{1,0:T(8,128)(2,1)S(1)} %collective-permute-done.4), channel_id=1, source_target_pairs={{0,4},{2,6},{4,0},{6,2},{8,12},{10,14},{12,8},{14,10},{16,20},{18,... | collective-permute-start | bytes 196616 | tf_op jit(solution)/shard_map/ppermute | solution.py:341
  18.3 1.5 %collective-permute-start.6 = (bf16[16,2048]{1,0:T(8,128)(2,1)S(1)}, bf16[16,2048]{1,0:T(8,128)(2,1)S(1)}, u32[]{:S(2)}, u32[]{:S(2)}) collective-permute-start(bf16[16,2048]{1,0:T(8,128)(2,1)S(1)} %collective-permute-done.4), channel_id=1, source_target_pairs={{0,8},{2,10},{4,12},{6,14},{8,0},{10,2},{12,4},{14,6},{16,24},{18,... | collective-permute-start | bytes 196616 | tf_op jit(solution)/shard_map/ppermute | solution.py:341
  20.0 0.8 %constant_dynamic-update-slice_fusion.4 = bf16[128,2048]{1,0:T(8,128)(2,1)S(1)} fusion(bf16[128,2048]{1,0:T(8,128)(2,1)S(1)} %constant_dynamic-update-slice_fusion.5, bf16[16,2048]{1,0:T(8,128)(2,1)} %param.19), kind=kLoop, calls=%fused_computation.61 | loop fusion | bytes 131072
  20.9 11.2 %early_heads.1.low_ref = bf16[16,1536,256]{2,1,0:T(8,128)(2,1)} custom-call(bf16[2048,16,256]{2,1,0:T(8,128)(2,1)} %head_ref.2), custom_call_target="tpu_custom_call" | custom-call | bytes 25165824 | tf_op jit(solution)/shard_map/early_heads/pallas_call | solution.py:421
  32.4 1.8 %collective-permute-done.8.refs_3_ = bf16[128,2048]{1,0:T(8,128)(2,1)S(1)} collective-permute-done((bf16[128,2048]{1,0:T(8,128)(2,1)S(1)}, bf16[128,2048]{1,0:T(8,128)(2,1)S(1)}, u32[]{:S(2)}, u32[]{:S(2)}) %collective-permute-start.8) | collective-permute-done | bytes 524320 | tf_op jit(solution)/shard_map/ppermute | solution.py:341
  34.2 10.7 %join.1 = (bf16[16,2048]{1,0:T(8,128)(2,1)S(1)}, s32[8,128]{1,0:T(8,128)S(1)}) custom-call(s32[2]{0:T(128)S(1)} %pad_add_fusion.1.place_ref, bf16[16,96,256]{2,1,0:T(8,128)(2,1)S(1)} %all-to-all-done.6.packed_ref, bf16[256,1024]{1,0:T(8,128)(2,1)S(1)} %copy-done, bf16[256,1024]{1,0:T(8,128)(2,1)S(1)} %collective-permute-done.refs_1_, ...), custom_call_target="tpu_custom_call" | custom-call | flops 12884901888 | bytes 2097152 | tf_op jit(solution)/shard_map/join/pallas_call | solution.py:435
  45.0 1.9 %collective-permute-start.11 = (bf16[16,2048]{1,0:T(8,128)(2,1)S(1)}, bf16[16,2048]{1,0:T(8,128)(2,1)S(1)}, u32[]{:S(2)}, u32[]{:S(2)}) collective-permute-start(bf16[16,2048]{1,0:T(8,128)(2,1)S(1)} %get-tuple-element.63), channel_id=1, source_target_pairs={{0,4},{2,6},{4,0},{6,2},{8,12},{10,14},{12,8},{14,10},{16,20},{18,... | collective-permute-start | bytes 196616 | tf_op jit(solution)/shard_map/ppermute | solution.py:341
  46.9 3.4 %collective-permute-start.9 = (bf16[16,2048]{1,0:T(8,128)(2,1)S(1)}, bf16[16,2048]{1,0:T(8,128)(2,1)S(1)}, u32[]{:S(2)}, u32[]{:S(2)}) collective-permute-start(bf16[16,2048]{1,0:T(8,128)(2,1)S(1)} %get-tuple-element.63), channel_id=1, source_target_pairs={{0,16},{2,18},{4,20},{6,22},{8,24},{10,26},{12,28},{14,30},{16,0},... | collective-permute-start | bytes 196616 | tf_op jit(solution)/shard_map/ppermute | solution.py:341
  50.3 0.4 collective-permute-start.12
  50.8 3.0 %collective-permute-start.13 = (bf16[16,2048]{1,0:T(8,128)(2,1)S(1)}, bf16[16,2048]{1,0:T(8,128)(2,1)S(1)}, u32[]{:S(2)}, u32[]{:S(2)}) collective-permute-start(bf16[16,2048]{1,0:T(8,128)(2,1)S(1)} %get-tuple-element.63), channel_id=1, source_target_pairs={{0,12},{2,14},{4,8},{6,10},{8,4},{10,6},{12,0},{14,2},{16,28},{18,... | collective-permute-start | bytes 196616 | tf_op jit(solution)/shard_map/ppermute | solution.py:341
  53.7 1.5 %collective-permute-start.10 = (s32[8,128]{1,0:T(8,128)S(1)}, s32[8,128]{1,0:T(8,128)S(1)}, u32[]{:S(2)}, u32[]{:S(2)}) collective-permute-start(s32[8,128]{1,0:T(8,128)S(1)} %get-tuple-element.64.refs_0_), channel_id=1, source_target_pairs={{0,1},{1,0},{2,3},{3,2},{4,5},{5,4},{6,7},{7,6},{8,9},{9,8},{10,11... | collective-permute-start | bytes 12296 | tf_op jit(solution)/shard_map/ppermute | solution.py:474
  55.7 1.9 %collective-permute-done.13 = bf16[16,2048]{1,0:T(8,128)(2,1)S(1)} collective-permute-done((bf16[16,2048]{1,0:T(8,128)(2,1)S(1)}, bf16[16,2048]{1,0:T(8,128)(2,1)S(1)}, u32[]{:S(2)}, u32[]{:S(2)}) %collective-permute-start.13) | collective-permute-done | bytes 65568 | tf_op jit(solution)/shard_map/ppermute | solution.py:341
  57.7 0.9 %collective-permute-start.15 = (bf16[16,2048]{1,0:T(8,128)(2,1)S(1)}, bf16[16,2048]{1,0:T(8,128)(2,1)S(1)}, u32[]{:S(2)}, u32[]{:S(2)}) collective-permute-start(bf16[16,2048]{1,0:T(8,128)(2,1)S(1)} %collective-permute-done.9.across_ref), channel_id=1, source_target_pairs={{0,8},{2,10},{4,12},{6,14},{8,0},{10,2},{12,4},{14,6},{16,24},{18,... | collective-permute-start | bytes 196616 | tf_op jit(solution)/shard_map/ppermute | solution.py:341
  58.6 0.9 %collective-permute-start.16 = (bf16[16,2048]{1,0:T(8,128)(2,1)S(1)}, bf16[16,2048]{1,0:T(8,128)(2,1)S(1)}, u32[]{:S(2)}, u32[]{:S(2)}) collective-permute-start(bf16[16,2048]{1,0:T(8,128)(2,1)S(1)} %collective-permute-done.9.across_ref), channel_id=1, source_target_pairs={{0,12},{2,14},{4,8},{6,10},{8,4},{10,6},{12,0},{14,2},{16,28},{18,... | collective-permute-start | bytes 196616 | tf_op jit(solution)/shard_map/ppermute | solution.py:341
  59.5 2.8 %late_heads.1 = (bf16[16,512,256]{2,1,0:T(8,128)(2,1)S(1)}, bf16[16,2048]{1,0:T(8,128)(2,1)S(1)}, s32[1]{0:T(128)}) custom-call(bf16[16,2048]{1,0:T(8,128)(2,1)S(1)} %collective-permute-done.9.across_ref, bf16[2048,16,256]{2,1,0:T(8,128)(2,1)} %head_ref.2, s32[8,128]{1,0:T(8,128)S(1)} %get-tuple-element.64.refs_0_, s32[8,128]{1,0:T(8,128)S(1)} %collective-permute-done.10.refs_1_), custom_call_target="tpu_custom_call" | custom-call | bytes 25165824 | tf_op jit(solution)/shard_map/late_heads/pallas_call | solution.py:476
  62.4 1.4 %collective-permute-done.16 = bf16[16,2048]{1,0:T(8,128)(2,1)S(1)} collective-permute-done((bf16[16,2048]{1,0:T(8,128)(2,1)S(1)}, bf16[16,2048]{1,0:T(8,128)(2,1)S(1)}, u32[]{:S(2)}, u32[]{:S(2)}) %collective-permute-start.16) | collective-permute-done | bytes 65568 | tf_op jit(solution)/shard_map/ppermute | solution.py:341
  64.5 1.2 %collective-permute-done.17.far_ref = bf16[128,2048]{1,0:T(8,128)(2,1)S(1)} collective-permute-done((bf16[128,2048]{1,0:T(8,128)(2,1)S(1)}, bf16[128,2048]{1,0:T(8,128)(2,1)S(1)}, u32[]{:S(2)}, u32[]{:S(2)}) %collective-permute-start.17) | collective-permute-done | bytes 524320 | tf_op jit(solution)/shard_map/ppermute | solution.py:341
  65.8 6.8 %decode.1 = bf16[16,16,16,256]{3,2,1,0:T(8,128)(2,1)} custom-call(s32[2]{0:T(128)S(1)} %pad_add_fusion.1.place_ref, bf16[128,2048]{1,0:T(8,128)(2,1)S(1)} %constant_dynamic-update-slice_fusion.8.near_ref, bf16[128,2048]{1,0:T(8,128)(2,1)S(1)} %collective-permute-done.17.far_ref, bf16[16,1536,256]{2,1,0:T(8,128)(2,1)S(1)} %bitcast.87, ...), custom_call_target="tpu_custom_call" | custom-call | flops 4294967296 | bytes 3145728 | tf_op jit(solution)/shard_map/decode/pallas_call | solution.py:492
  (65 shorter events, 1.7 us)
Async XLA Ops:
  0.0 34.2 %copy-start = (bf16[256,1024]{1,0:T(8,128)(2,1)S(1)}, bf16[256,1024]{1,0:T(8,128)(2,1)}, u32[]{:S(2)}) copy-start(bf16[256,1024]{1,0:T(8,128)(2,1)} %refs_0_.1) | copy-start | bytes 1572868
  0.0 34.2 %copy-start.2 = (bf16[16,2048]{1,0:T(8,128)(2,1)S(1)}, bf16[16,2048]{1,0:T(8,128)(2,1)}, u32[]{:S(2)}) copy-start(bf16[16,2048]{1,0:T(8,128)(2,1)} %refs_5_.1) | copy-start | bytes 196612
  0.0 34.2 %copy-start.9 = (f32[16,64]{1,0:T(8,128)S(1)}, f32[16,64]{1,0:T(8,128)}, u32[]{:S(2)}) copy-start(f32[16,64]{1,0:T(8,128)} %refs_7_.1) | copy-start | bytes 12292
  0.0 34.2 %copy-start.11 = (f32[2048]{0:T(1024)S(1)}, f32[2048]{0:T(1024)}, u32[]{:S(2)}) copy-start(f32[2048]{0:T(1024)} %param.23) | copy-start | bytes 24580
  0.0 34.2 %copy-start.15 = (s32[256]{0:T(256)S(1)}, s32[256]{0:T(256)}, u32[]{:S(2)}) copy-start(s32[256]{0:T(256)} %param.16) | copy-start | bytes 3076
  3.4 13.0 %collective-permute-start.4 = (bf16[16,2048]{1,0:T(8,128)(2,1)}, bf16[16,2048]{1,0:T(8,128)(2,1)S(1)}, u32[]{:S(2)}, u32[]{:S(2)}) collective-permute-start(bf16[16,2048]{1,0:T(8,128)(2,1)} %param.19), channel_id=1, source_target_pairs={{0,16},{2,18},{4,20},{6,22},{8,24},{10,26},{12,28},{14,30},{16,0},... | collective-permute-start | bytes 196616 | tf_op jit(solution)/shard_map/ppermute | solution.py:341
  7.4 10.8 %collective-permute-start.1 = (bf16[16,2048]{1,0:T(8,128)(2,1)}, bf16[16,2048]{1,0:T(8,128)(2,1)S(1)}, u32[]{:S(2)}, u32[]{:S(2)}) collective-permute-start(bf16[16,2048]{1,0:T(8,128)(2,1)} %param.19), channel_id=1, source_target_pairs={{0,4},{2,6},{4,0},{6,2},{8,12},{10,14},{12,8},{14,10},{16,20},{18,... | collective-permute-start | bytes 196616 | tf_op jit(solution)/shard_map/ppermute | solution.py:341
  9.0 10.8 %collective-permute-start.2 = (bf16[16,2048]{1,0:T(8,128)(2,1)}, bf16[16,2048]{1,0:T(8,128)(2,1)S(1)}, u32[]{:S(2)}, u32[]{:S(2)}) collective-permute-start(bf16[16,2048]{1,0:T(8,128)(2,1)} %param.19), channel_id=1, source_target_pairs={{0,8},{2,10},{4,12},{6,14},{8,0},{10,2},{12,4},{14,6},{16,24},{18,... | collective-permute-start | bytes 196616 | tf_op jit(solution)/shard_map/ppermute | solution.py:341
  10.5 9.5 %collective-permute-start.3 = (bf16[16,2048]{1,0:T(8,128)(2,1)}, bf16[16,2048]{1,0:T(8,128)(2,1)S(1)}, u32[]{:S(2)}, u32[]{:S(2)}) collective-permute-start(bf16[16,2048]{1,0:T(8,128)(2,1)} %param.19), channel_id=1, source_target_pairs={{0,12},{2,14},{4,8},{6,10},{8,4},{10,6},{12,0},{14,2},{16,28},{18,... | collective-permute-start | bytes 196616 | tf_op jit(solution)/shard_map/ppermute | solution.py:341
  10.9 23.3 %all-to-all-start.6 = ((bf16[16,96,256]{2,1,0:T(8,128)(2,1)}), bf16[16,96,256]{2,1,0:T(8,128)(2,1)S(1)}, u32[]{:S(2)}, u32[]{:S(2)}) async-start(bf16[16,96,256]{2,1,0:T(8,128)(2,1)} %pack.1), calls=%async_computation.6 | async-start | bytes 1572864 | tf_op jit(solution)/shard_map/all_to_all | solution.py:409
  14.9 17.5 %collective-permute-start = (bf16[256,1024]{1,0:T(8,128)(2,1)}, bf16[256,1024]{1,0:T(8,128)(2,1)S(1)}, u32[]{:S(2)}, u32[]{:S(2)}) collective-permute-start(bf16[256,1024]{1,0:T(8,128)(2,1)} %refs_0_.1), channel_id=1, source_target_pairs={{0,1},{1,0},{2,3},{3,2},{4,5},{5,4},{6,7},{7,6},{8,9},{9,8},{10,11... | collective-permute-start | bytes 1572872 | tf_op jit(solution)/shard_map/ppermute | solution.py:413
  16.4 15.7 %collective-permute-start.5 = (bf16[16,2048]{1,0:T(8,128)(2,1)S(1)}, bf16[16,2048]{1,0:T(8,128)(2,1)S(1)}, u32[]{:S(2)}, u32[]{:S(2)}) collective-permute-start(bf16[16,2048]{1,0:T(8,128)(2,1)S(1)} %collective-permute-done.4), channel_id=1, source_target_pairs={{0,4},{2,6},{4,0},{6,2},{8,12},{10,14},{12,8},{14,10},{16,20},{18,... | collective-permute-start | bytes 196616 | tf_op jit(solution)/shard_map/ppermute | solution.py:341
  18.3 13.9 %collective-permute-start.6 = (bf16[16,2048]{1,0:T(8,128)(2,1)S(1)}, bf16[16,2048]{1,0:T(8,128)(2,1)S(1)}, u32[]{:S(2)}, u32[]{:S(2)}) collective-permute-start(bf16[16,2048]{1,0:T(8,128)(2,1)S(1)} %collective-permute-done.4), channel_id=1, source_target_pairs={{0,8},{2,10},{4,12},{6,14},{8,0},{10,2},{12,4},{14,6},{16,24},{18,... | collective-permute-start | bytes 196616 | tf_op jit(solution)/shard_map/ppermute | solution.py:341
  19.8 12.4 %collective-permute-start.7 = (bf16[16,2048]{1,0:T(8,128)(2,1)S(1)}, bf16[16,2048]{1,0:T(8,128)(2,1)S(1)}, u32[]{:S(2)}, u32[]{:S(2)}) collective-permute-start(bf16[16,2048]{1,0:T(8,128)(2,1)S(1)} %collective-permute-done.4), channel_id=1, source_target_pairs={{0,12},{2,14},{4,8},{6,10},{8,4},{10,6},{12,0},{14,2},{16,28},{18,... | collective-permute-start | bytes 196616 | tf_op jit(solution)/shard_map/ppermute | solution.py:341
  32.2 2.0 %collective-permute-start.8 = (bf16[128,2048]{1,0:T(8,128)(2,1)S(1)}, bf16[128,2048]{1,0:T(8,128)(2,1)S(1)}, u32[]{:S(2)}, u32[]{:S(2)}) collective-permute-start(bf16[128,2048]{1,0:T(8,128)(2,1)S(1)} %constant_dynamic-update-slice_fusion.refs_2_), channel_id=1, source_target_pairs={{0,2},{2,0},{4,6},{6,4},{8,10},{10,8},{12,14},{14,12},{16,18},{18,... | collective-permute-start | bytes 1572872 | tf_op jit(solution)/shard_map/ppermute | solution.py:341
  45.0 10.2 %collective-permute-start.11 = (bf16[16,2048]{1,0:T(8,128)(2,1)S(1)}, bf16[16,2048]{1,0:T(8,128)(2,1)S(1)}, u32[]{:S(2)}, u32[]{:S(2)}) collective-permute-start(bf16[16,2048]{1,0:T(8,128)(2,1)S(1)} %get-tuple-element.63), channel_id=1, source_target_pairs={{0,4},{2,6},{4,0},{6,2},{8,12},{10,14},{12,8},{14,10},{16,20},{18,... | collective-permute-start | bytes 196616 | tf_op jit(solution)/shard_map/ppermute | solution.py:341
  46.9 8.3 %collective-permute-start.9 = (bf16[16,2048]{1,0:T(8,128)(2,1)S(1)}, bf16[16,2048]{1,0:T(8,128)(2,1)S(1)}, u32[]{:S(2)}, u32[]{:S(2)}) collective-permute-start(bf16[16,2048]{1,0:T(8,128)(2,1)S(1)} %get-tuple-element.63), channel_id=1, source_target_pairs={{0,16},{2,18},{4,20},{6,22},{8,24},{10,26},{12,28},{14,30},{16,0},... | collective-permute-start | bytes 196616 | tf_op jit(solution)/shard_map/ppermute | solution.py:341
  50.3 5.3 %collective-permute-start.12 = (bf16[16,2048]{1,0:T(8,128)(2,1)S(1)}, bf16[16,2048]{1,0:T(8,128)(2,1)S(1)}, u32[]{:S(2)}, u32[]{:S(2)}) collective-permute-start(bf16[16,2048]{1,0:T(8,128)(2,1)S(1)} %get-tuple-element.63), channel_id=1, source_target_pairs={{0,8},{2,10},{4,12},{6,14},{8,0},{10,2},{12,4},{14,6},{16,24},{18,... | collective-permute-start | bytes 196616 | tf_op jit(solution)/shard_map/ppermute | solution.py:341
  50.8 6.8 %collective-permute-start.13 = (bf16[16,2048]{1,0:T(8,128)(2,1)S(1)}, bf16[16,2048]{1,0:T(8,128)(2,1)S(1)}, u32[]{:S(2)}, u32[]{:S(2)}) collective-permute-start(bf16[16,2048]{1,0:T(8,128)(2,1)S(1)} %get-tuple-element.63), channel_id=1, source_target_pairs={{0,12},{2,14},{4,8},{6,10},{8,4},{10,6},{12,0},{14,2},{16,28},{18,... | collective-permute-start | bytes 196616 | tf_op jit(solution)/shard_map/ppermute | solution.py:341
  53.7 5.8 %collective-permute-start.10 = (s32[8,128]{1,0:T(8,128)S(1)}, s32[8,128]{1,0:T(8,128)S(1)}, u32[]{:S(2)}, u32[]{:S(2)}) collective-permute-start(s32[8,128]{1,0:T(8,128)S(1)} %get-tuple-element.64.refs_0_), channel_id=1, source_target_pairs={{0,1},{1,0},{2,3},{3,2},{4,5},{5,4},{6,7},{7,6},{8,9},{9,8},{10,11... | collective-permute-start | bytes 12296 | tf_op jit(solution)/shard_map/ppermute | solution.py:474
  55.3 7.1 %collective-permute-start.14 = (bf16[16,2048]{1,0:T(8,128)(2,1)S(1)}, bf16[16,2048]{1,0:T(8,128)(2,1)S(1)}, u32[]{:S(2)}, u32[]{:S(2)}) collective-permute-start(bf16[16,2048]{1,0:T(8,128)(2,1)S(1)} %collective-permute-done.9.across_ref), channel_id=1, source_target_pairs={{0,4},{2,6},{4,0},{6,2},{8,12},{10,14},{12,8},{14,10},{16,20},{18,... | collective-permute-start | bytes 196616 | tf_op jit(solution)/shard_map/ppermute | solution.py:341
  57.7 4.7 %collective-permute-start.15 = (bf16[16,2048]{1,0:T(8,128)(2,1)S(1)}, bf16[16,2048]{1,0:T(8,128)(2,1)S(1)}, u32[]{:S(2)}, u32[]{:S(2)}) collective-permute-start(bf16[16,2048]{1,0:T(8,128)(2,1)S(1)} %collective-permute-done.9.across_ref), channel_id=1, source_target_pairs={{0,8},{2,10},{4,12},{6,14},{8,0},{10,2},{12,4},{14,6},{16,24},{18,... | collective-permute-start | bytes 196616 | tf_op jit(solution)/shard_map/ppermute | solution.py:341
  58.6 5.2 %collective-permute-start.16 = (bf16[16,2048]{1,0:T(8,128)(2,1)S(1)}, bf16[16,2048]{1,0:T(8,128)(2,1)S(1)}, u32[]{:S(2)}, u32[]{:S(2)}) collective-permute-start(bf16[16,2048]{1,0:T(8,128)(2,1)S(1)} %collective-permute-done.9.across_ref), channel_id=1, source_target_pairs={{0,12},{2,14},{4,8},{6,10},{8,4},{10,6},{12,0},{14,2},{16,28},{18,... | collective-permute-start | bytes 196616 | tf_op jit(solution)/shard_map/ppermute | solution.py:341
  63.8 2.0 %collective-permute-start.17 = (bf16[128,2048]{1,0:T(8,128)(2,1)S(1)}, bf16[128,2048]{1,0:T(8,128)(2,1)S(1)}, u32[]{:S(2)}, u32[]{:S(2)}) collective-permute-start(bf16[128,2048]{1,0:T(8,128)(2,1)S(1)} %constant_dynamic-update-slice_fusion.8.near_ref), channel_id=1, source_target_pairs={{0,2},{2,0},{4,6},{6,4},{8,10},{10,8},{12,14},{14,12},{16,18},{18,... | collective-permute-start | bytes 1572872 | tf_op jit(solution)/shard_map/ppermute | solution.py:341
  (8 other events, 192.4 us)
